TPU v7x, 512 devices: a whole 4x8x8 slice. The times are simulated.
512 devices in a mesh: lon: 32 (over z_lo, y, core), lat: 16 (over z_hi, x).
Axes of the slice: x: 4, y: 8, z: 8 (z_hi: 4, z_lo: 2; z = z_hi * 2 + z_lo), core: 2. Of those that a mesh axis runs over, the one named last changes fastest.
Arguments:
- tokens: bfloat16 [384, 128, 1024], P('lon', 'lat'), may hold values from -6 to 6
- query_local: bfloat16 [384, 128, 1024], P('lon', 'lat'), may hold values from -21 to 21, as said below
- key_local: bfloat16 [384, 128, 1024], P('lon', 'lat'), may hold values from -21 to 21, as said below
- value_local: bfloat16 [384, 128, 1024], P('lon', 'lat'), may hold values from -6 to 6
- position_bias: float32 [16, 13, 13], replicated, may hold values from -4 to 4
- output_weight: bfloat16 [1024, 1024], P('lat'), may hold values from -0.1875 to 0.1875
- norm_gain: float32 [1024], replicated, may hold values from 0.1 to 1.9
- global_weight: bfloat16 [1024, 3072], P('lat'), may hold values from -1 to 1
Outputs:
- hidden: bfloat16 [384, 128, 1024], P('lon', 'lat')
- attended: bfloat16 [384, 128, 1024], P('lon', 'lat')
Inputs may be any that keep to these rules, and one draw needn't show every extreme that they name: `query_local`: entries of the neighbourhood queries and keys. `key_local`: entries of the neighbourhood queries and keys.
All inputs are finite; a program needn't handle non-finite values.
Results may differ from a plain program's by a relative error of at most 0.015.
Values may be sent and summed in bfloat16 or wider, within the bound.
No kernel may reach another device: no remote copies, remote signals or barrier semaphores. Data moves between devices by JAX's collectives and lax.ppermute only.
A program may use at most 64 MiB of HBM per device.

v0:
```python
import math
import jax
import jax.numpy as jnp
from jax import lax
from jax.sharding import PartitionSpec as P

STEPS = 4


def extended(block, sides, width):
    for axis, dim in sides:
        count = lax.axis_size(axis)
        forward = [(i, i + 1) for i in range(count - 1)]
        forward.append((count - 1, 0))
        backward = [(target, source) for source, target in forward]
        low = lax.ppermute(
            lax.slice_in_dim(block, block.shape[dim] - width, None, axis=dim), axis, forward
        )
        high = lax.ppermute(lax.slice_in_dim(block, 0, width, axis=dim), axis, backward)
        block = jnp.concatenate([low, block, high], axis=dim)
    return block


def from_behind(x, axis, by):
    count = lax.axis_size(axis)
    return lax.ppermute(x, axis, [(i, (i + by) % count) for i in range(count)])


def offset_table(cells, span, window):
    query_pos = lax.broadcasted_iota(jnp.int32, (cells, span, window), 0)
    key_pos = lax.broadcasted_iota(jnp.int32, (cells, span, window), 1)
    offset = lax.broadcasted_iota(jnp.int32, (cells, span, window), 2)
    return (key_pos - query_pos == offset).astype(jnp.float32)


def fold_rows(left, weight_rows):
    return jnp.dot(left, weight_rows, preferred_element_type=jnp.float32)


def block_merge(carry_state, query_heads, key_block, score_scale):
    running_max, denominator, accumulated = carry_state
    head_count = query_heads.shape[1]
    head_size = query_heads.shape[2]
    keys_part = key_block[0].reshape(key_block.shape[1], head_count, head_size)
    values_part = key_block[1].reshape(key_block.shape[1], head_count, head_size)
    scores = (
        jnp.einsum("qhd,khd->hqk", query_heads, keys_part, preferred_element_type=jnp.float32)
        * score_scale
    )
    new_max = jnp.maximum(running_max, jnp.max(scores, axis=2))
    factor = jnp.exp(running_max - new_max)
    weights = jnp.exp(scores - new_max[:, :, None])
    denominator = denominator * factor + jnp.sum(weights, axis=2)
    weighted = jnp.einsum(
        "hqk,khd->hqd",
        weights.astype(jnp.bfloat16),
        values_part,
        preferred_element_type=jnp.float32,
    )
    accumulated = accumulated * factor[:, :, None] + weighted
    return (new_max, denominator, accumulated)


def body(
    tokens,
    query_local,
    key_local,
    value_local,
    position_bias,
    output_weight,
    norm_gain,
    global_weight,
):
    lon_cells, lat_cells, model_width = tokens.shape
    head_count = position_bias.shape[0]
    radius = (position_bias.shape[1] - 1) // 2
    window = 2 * radius + 1
    head_size = model_width // head_count
    score_scale = 1.0 / math.sqrt(head_size)
    token_count = lon_cells * lat_cells
    lon_span = lon_cells + 2 * radius
    lat_span = lat_cells + 2 * radius
    stacked = jnp.stack([key_local, value_local])
    padded = extended(stacked, (("lon", 1), ("lat", 2)), radius)
    window_keys = padded[0].reshape(lon_span * lat_span, head_count, head_size)
    window_values = padded[1].reshape(lon_span * lat_span, head_count, head_size)
    query_heads = query_local.reshape(token_count, head_count, head_size)
    lon_table = offset_table(lon_cells, lon_span, window)
    lat_table = offset_table(lat_cells, lat_span, window)
    lat_start = lax.axis_index("lat") * lat_cells
    lat_total = lat_cells * lax.axis_size("lat")
    lat_global = lat_start + jnp.arange(lat_span, dtype=jnp.int32) - radius
    lat_inside = (lat_global >= 0) & (lat_global < lat_total)
    lon_near = jnp.sum(lon_table, axis=2) > 0.5
    lat_near = (jnp.sum(lat_table, axis=2) > 0.5) & lat_inside[None, :]
    allowed = (lon_near[:, None, :, None] & lat_near[None, :, None, :]).reshape(
        token_count, lon_span * lat_span
    )

    def one_head(operands):
        query_one, key_one, value_one, bias_one = operands
        bias_lat = jnp.einsum("ab,jkb->ajk", bias_one, lat_table, precision=lax.Precision.HIGHEST)
        bias_full = jnp.einsum(
            "ajk,ila->ijlk", bias_lat, lon_table, precision=lax.Precision.HIGHEST
        )
        bias_full = bias_full.reshape(token_count, lon_span * lat_span)
        scores = jnp.einsum("qd,kd->qk", query_one, key_one, preferred_element_type=jnp.float32)
        scores = jnp.where(allowed, scores * score_scale + bias_full, -1e30)
        largest = jnp.max(scores, axis=1, keepdims=True)
        weights = jnp.exp(scores - largest)
        denominator = jnp.sum(weights, axis=1, keepdims=True)
        weighted = jnp.dot(
            weights.astype(jnp.bfloat16), value_one, preferred_element_type=jnp.float32
        )
        return (weighted / denominator).astype(jnp.bfloat16)

    head_outputs = lax.map(
        one_head,
        (
            jnp.transpose(query_heads, (1, 0, 2)),
            jnp.transpose(window_keys, (1, 0, 2)),
            jnp.transpose(window_values, (1, 0, 2)),
            position_bias,
        ),
    )
    local_out = jnp.transpose(head_outputs, (1, 0, 2)).reshape(token_count, model_width)
    flat_tokens = tokens.reshape(token_count, model_width)
    projected = fold_rows(local_out, lax.all_gather(output_weight, "lat", axis=0, tiled=True))
    hidden = (flat_tokens.astype(jnp.float32) + projected).astype(jnp.bfloat16)
    widened_hidden = hidden.astype(jnp.float32)
    inverse = lax.rsqrt(jnp.mean(widened_hidden * widened_hidden, axis=1, keepdims=True) + 1e-06)
    normed = (widened_hidden * inverse * norm_gain).astype(jnp.bfloat16)
    triple = fold_rows(normed, lax.all_gather(global_weight, "lat", axis=0, tiled=True))
    triple = triple.astype(jnp.bfloat16)
    global_query = triple[:, :model_width].reshape(token_count, head_count, head_size)
    key_pair = jnp.stack([triple[:, model_width : 2 * model_width], triple[:, 2 * model_width :]])
    carry_state = (
        jnp.full((head_count, token_count), -1e30, jnp.float32),
        jnp.zeros((head_count, token_count), jnp.float32),
        jnp.zeros((head_count, token_count, head_size), jnp.float32),
    )
    carry_state = block_merge(carry_state, global_query, key_pair, score_scale)
    travelling = key_pair
    for hop_index in range(STEPS):
        travelling = from_behind(travelling, ("lon", "lat"), 1)
        carry_state = block_merge(carry_state, global_query, travelling, score_scale)
    running_max, denominator, accumulated = carry_state
    attended = accumulated / denominator[:, :, None]
    attended = (
        jnp.transpose(attended, (1, 0, 2))
        .reshape(lon_cells, lat_cells, model_width)
        .astype(jnp.bfloat16)
    )
    return (hidden.reshape(lon_cells, lat_cells, model_width), attended)


def solution(mesh):
    return jax.shard_map(
        body,
        mesh=mesh,
        in_specs=(
            P("lon", "lat", None),
            P("lon", "lat", None),
            P("lon", "lat", None),
            P("lon", "lat", None),
            P(),
            P("lat", None),
            P(),
            P("lat", None),
        ),
        out_specs=(P("lon", "lat", None), P("lon", "lat", None)),
        check_vma=False,
    )
```

profile of v0, /device:TPU:313, one launch (start us, length us, event | category | flops | bytes accessed | tf_op | source)
XLA Modules:
  0.0 309.6 jit_solution(16309423687903335286)
XLA Ops:
  7.9 1.2 copy_bitcast_fusion.2
  9.3 2.9 collective-permute-start
  12.2 2.1 collective-permute-start.1
  14.3 1.2 collective-permute-done
  15.5 6.6 %collective-permute-done.1 = bf16[2,6,8,1024]{3,1,2,0:T(8,128)(2,1)S(1)} collective-permute-done((bf16[2,6,8,1024]{3,1,2,0:T(8,128)(2,1)S(1)}, bf16[2,6,8,1024]{3,1,2,0:T(8,128)(2,1)S(1)}, u32[]{:S(2)}, u32[]{:S(2)}) %collective-permute-start.1) | collective-permute-done | bytes 196640 | tf_op jit(solution)/shard_map/ppermute | solution.py:19
  23.5 3.1 %collective-permute-start.2 = (bf16[2,24,6,1024]{3,1,2,0:T(8,128)(2,1)}, bf16[2,24,6,1024]{3,1,2,0:T(8,128)(2,1)S(1)}, u32[]{:S(2)}, u32[]{:S(2)}) collective-permute-start(bf16[2,24,6,1024]{3,1,2,0:T(8,128)(2,1)} %get-tuple-element.126), channel_id=1, source_target_pairs={{0,1},{1,2},{2,3},{3,4},{4,5},{5,6},{6,7},{7,8},{8,9},{9,10},{10,1... | collective-permute-start | bytes 1769480 | tf_op jit(solution)/shard_map/ppermute | solution.py:16
  26.6 6.4 %collective-permute-start.3 = (bf16[2,24,6,1024]{3,1,2,0:T(8,128)(2,1)S(1)}, bf16[2,24,6,1024]{3,1,2,0:T(8,128)(2,1)}, u32[]{:S(2)}, u32[]{:S(2)}) collective-permute-start(bf16[2,24,6,1024]{3,1,2,0:T(8,128)(2,1)S(1)} %get-tuple-element.127), channel_id=1, source_target_pairs={{1,0},{2,1},{3,2},{4,3},{5,4},{6,5},{7,6},{8,7},{9,8},{10,9},{11,1... | collective-permute-start | bytes 1769480 | tf_op jit(solution)/shard_map/ppermute | solution.py:19
  33.6 26.1 %collective-permute-done.2 = bf16[2,24,6,1024]{3,1,2,0:T(8,128)(2,1)S(1)} collective-permute-done((bf16[2,24,6,1024]{3,1,2,0:T(8,128)(2,1)}, bf16[2,24,6,1024]{3,1,2,0:T(8,128)(2,1)S(1)}, u32[]{:S(2)}, u32[]{:S(2)}) %collective-permute-start.2) | collective-permute-done | bytes 589856 | tf_op jit(solution)/shard_map/ppermute | solution.py:16
  59.6 1.6 pad_maximum_fusion
  62.9 1.3 reshape_squeeze.30
  64.3 1.8 copy.86
  66.7 1.3 reshape_squeeze.31
  68.0 1.8 copy.88
  69.8 103.0 %while.11 = (s32[]{:T(128)}, bf16[16,96,64]{1,2,0:T(8,128)(2,1)S(1)}, bf16[16,96,64]{2,1,0:T(8,128)(2,1)S(1)}, bf16[16,480,64]{2,1,0:T(8,128)(2,1)}, f32[16,13,1...) while((s32[]{:T(128)}, ...), condition=%wide.region_5.6_spmd.clone, body=%wide.region_2.5_spmd.clone.sunk | while | flops 19753728 | bytes 2181005 | solution.py:117
  73.7 1.2 fusion.121
  75.1 1.2 fusion.123
  80.1 1.2 fusion.121
  81.5 1.2 fusion.123
  86.5 1.2 fusion.121
  87.9 1.2 fusion.123
  93.0 1.2 fusion.121
  94.4 1.2 fusion.123
  99.4 1.2 fusion.121
  100.8 1.2 fusion.123
  105.8 1.2 fusion.121
  107.2 1.2 fusion.123
  109.5 1.1 convolution_bitcast_fusion.10
  112.3 1.2 fusion.121
  113.7 1.2 fusion.123
  115.9 1.1 convolution_bitcast_fusion.10
  118.7 1.2 fusion.121
  120.1 1.2 fusion.123
  125.1 1.2 fusion.121
  126.5 1.2 fusion.123
  128.8 1.1 convolution_bitcast_fusion.10
  131.6 1.2 fusion.121
  133.0 1.2 fusion.123
  138.0 1.2 fusion.121
  139.4 1.2 fusion.123
  144.5 1.2 fusion.121
  145.9 1.2 fusion.123
  150.9 1.2 fusion.121
  152.3 1.2 fusion.123
  157.3 1.2 fusion.121
  158.7 1.2 fusion.123
  163.8 1.2 fusion.121
  165.2 1.2 fusion.123
  170.2 1.2 fusion.121
  171.6 1.2 fusion.123
  172.8 2.3 fusion.48
  175.1 17.7 %all-gather.5.cloned.1.call-done = bf16[1024,3072]{1,0:T(8,128)(2,1)} async-done(((bf16[64,3072]{1,0:T(8,128)(2,1)}), bf16[1024,3072]{1,0:T(8,128)(2,1)}) %all-gather.5.cloned.1.call-update) | async-done | bytes 6291472 | tf_op jit(solution)/shard_map/all_gather | solution.py:133
  192.9 4.0 %convolution_convert_fusion = bf16[96,3072]{1,0:T(8,128)(2,1)S(1)} fusion(bf16[1024,3072]{1,0:T(8,128)(2,1)} %all-gather.5.cloned.1.call-done, bf16[96,1024]{1,0:T(8,128)(2,1)S(1)} %get-tuple-element.147, f32[1024]{0:T(1024)S(1)} %copy-done.10, f32[96]{0:T(128)S(1)} %add_rsqrt_fusion), kind=kOutput, calls=%fused_computation.32 | convolution fusion | flops 604667904 | bytes 7082368 | tf_op jit(solution)/shard_map/dot_general | solution.py:37
  197.0 3.2 %collective-permute-start.4 = (bf16[2,96,1024]{2,1,0:T(8,128)(2,1)S(1)}, bf16[2,96,1024]{2,1,0:T(8,128)(2,1)S(1)}, u32[]{:S(2)}, u32[]{:S(2)}) collective-permute-start(bf16[2,96,1024]{2,1,0:T(8,128)(2,1)S(1)} %pad_maximum_fusion.2), channel_id=1, source_target_pairs={{0,1},{1,2},{2,3},{3,4},{4,5},{5,6},{6,7},{7,8},{8,9},{9,10},{10,1... | collective-permute-start | bytes 1179656 | tf_op jit(solution)/shard_map/ppermute | solution.py:26
  201.8 20.7 %collective-permute-done.4 = bf16[2,96,1024]{2,1,0:T(8,128)(2,1)S(1)} collective-permute-done((bf16[2,96,1024]{2,1,0:T(8,128)(2,1)S(1)}, bf16[2,96,1024]{2,1,0:T(8,128)(2,1)S(1)}, u32[]{:S(2)}, u32[]{:S(2)}) %collective-permute-start.4) | collective-permute-done | bytes 393248 | tf_op jit(solution)/shard_map/ppermute | solution.py:26
  222.5 1.9 collective-permute-start.5
  225.8 22.2 %collective-permute-done.5 = bf16[2,96,1024]{2,1,0:T(8,128)(2,1)} collective-permute-done((bf16[2,96,1024]{2,1,0:T(8,128)(2,1)S(1)}, bf16[2,96,1024]{2,1,0:T(8,128)(2,1)}, u32[]{:S(2)}, u32[]{:S(2)}) %collective-permute-start.5) | collective-permute-done | bytes 393248 | tf_op jit(solution)/shard_map/ppermute | solution.py:26
  247.9 1.9 collective-permute-start.6
  252.3 17.8 %collective-permute-done.6 = bf16[2,96,1024]{2,1,0:T(8,128)(2,1)} collective-permute-done((bf16[2,96,1024]{2,1,0:T(8,128)(2,1)}, bf16[2,96,1024]{2,1,0:T(8,128)(2,1)}, u32[]{:S(2)}, u32[]{:S(2)}) %collective-permute-start.6) | collective-permute-done | bytes 393248 | tf_op jit(solution)/shard_map/ppermute | solution.py:26
  270.1 2.1 collective-permute-start.7
  274.9 1.3 fusion.85
  276.2 15.4 %collective-permute-done.7 = bf16[2,96,1024]{2,1,0:T(8,128)(2,1)} collective-permute-done((bf16[2,96,1024]{2,1,0:T(8,128)(2,1)}, bf16[2,96,1024]{2,1,0:T(8,128)(2,1)}, u32[]{:S(2)}, u32[]{:S(2)}) %collective-permute-start.7) | collective-permute-done | bytes 393248 | tf_op jit(solution)/shard_map/ppermute | solution.py:26
  291.6 1.8 fusion.80
  293.3 1.8 copy.102
  295.1 2.1 fusion.84
  (200 shorter events, 79.2 us)
Async XLA Ops:
  7.2 165.7 %all-gather.3.cloned.1.call-start = ((), (), s32[]{:S(2)}) async-start(), calls=%async_computation | async-start | bytes 2228224 | tf_op jit(solution)/shard_map/all_gather | solution.py:128
  7.9 185.0 %all-gather.5.cloned.1.call-start = ((), (), s32[]{:S(2)}) async-start(), calls=%async_computation.1 | async-start | bytes 6684672 | tf_op jit(solution)/shard_map/all_gather | solution.py:133
  9.3 6.2 %collective-permute-start = (bf16[2,6,8,1024]{3,1,2,0:T(8,128)(2,1)S(1)}, bf16[2,6,8,1024]{3,1,2,0:T(8,128)(2,1)S(1)}, u32[]{:S(2)}, u32[]{:S(2)}) collective-permute-start(bf16[2,6,8,1024]{3,1,2,0:T(8,128)(2,1)S(1)} %get-tuple-element.133), channel_id=1, source_target_pairs={{0,16},{16,32},{32,48},{48,64},{64,80},{80,96},{96,112},{112,128},... | collective-permute-start | bytes 589832 | tf_op jit(solution)/shard_map/ppermute | solution.py:16
  12.2 20.9 %copy-start.9 = (bf16[12,8,1024]{2,1,0:T(8,128)(2,1)S(1)}, bf16[12,8,1024]{2,1,0:T(8,128)(2,1)}, u32[]{:S(2)}) copy-start(bf16[12,8,1024]{2,1,0:T(8,128)(2,1)} %param.11) | copy-start | bytes 589828
  12.2 9.9 %collective-permute-start.1 = (bf16[2,6,8,1024]{3,1,2,0:T(8,128)(2,1)S(1)}, bf16[2,6,8,1024]{3,1,2,0:T(8,128)(2,1)S(1)}, u32[]{:S(2)}, u32[]{:S(2)}) collective-permute-start(bf16[2,6,8,1024]{3,1,2,0:T(8,128)(2,1)S(1)} %get-tuple-element.134), channel_id=1, source_target_pairs={{16,0},{32,16},{48,32},{64,48},{80,64},{96,80},{112,96},{128,112},... | collective-permute-start | bytes 589832 | tf_op jit(solution)/shard_map/ppermute | solution.py:19
  23.5 36.1 %collective-permute-start.2 = (bf16[2,24,6,1024]{3,1,2,0:T(8,128)(2,1)}, bf16[2,24,6,1024]{3,1,2,0:T(8,128)(2,1)S(1)}, u32[]{:S(2)}, u32[]{:S(2)}) collective-permute-start(bf16[2,24,6,1024]{3,1,2,0:T(8,128)(2,1)} %get-tuple-element.126), channel_id=1, source_target_pairs={{0,1},{1,2},{2,3},{3,4},{4,5},{5,6},{6,7},{7,8},{8,9},{9,10},{10,1... | collective-permute-start | bytes 1769480 | tf_op jit(solution)/shard_map/ppermute | solution.py:16
  26.6 33.0 %collective-permute-start.3 = (bf16[2,24,6,1024]{3,1,2,0:T(8,128)(2,1)S(1)}, bf16[2,24,6,1024]{3,1,2,0:T(8,128)(2,1)}, u32[]{:S(2)}, u32[]{:S(2)}) collective-permute-start(bf16[2,24,6,1024]{3,1,2,0:T(8,128)(2,1)S(1)} %get-tuple-element.127), channel_id=1, source_target_pairs={{1,0},{2,1},{3,2},{4,3},{5,4},{6,5},{7,6},{8,7},{9,8},{10,9},{11,1... | collective-permute-start | bytes 1769480 | tf_op jit(solution)/shard_map/ppermute | solution.py:19
  64.3 1.9 copy-start
  68.0 1.8 copy-start.7
  69.8 103.1 %copy-start.8 = (bf16[12,8,1024]{2,1,0:T(8,128)(2,1)S(1)}, bf16[12,8,1024]{2,1,0:T(8,128)(2,1)}, u32[]{:S(2)}) copy-start(bf16[12,8,1024]{2,1,0:T(8,128)(2,1)} %param.10) | copy-start | bytes 589828
  172.8 20.1 %copy-start.10 = (f32[1024]{0:T(1024)S(1)}, f32[1024]{0:T(1024)}, u32[]{:S(2)}) copy-start(f32[1024]{0:T(1024)} %param.16) | copy-start | bytes 12292
  175.1 21.7 %copy-start.6 = (bf16[96,1024]{1,0:T(8,128)(2,1)}, bf16[96,1024]{1,0:T(8,128)(2,1)S(1)}, u32[]{:S(2)}) copy-start(bf16[96,1024]{1,0:T(8,128)(2,1)S(1)} %get-tuple-element.147) | copy-start | bytes 589828
  197.0 25.4 %collective-permute-start.4 = (bf16[2,96,1024]{2,1,0:T(8,128)(2,1)S(1)}, bf16[2,96,1024]{2,1,0:T(8,128)(2,1)S(1)}, u32[]{:S(2)}, u32[]{:S(2)}) collective-permute-start(bf16[2,96,1024]{2,1,0:T(8,128)(2,1)S(1)} %pad_maximum_fusion.2), channel_id=1, source_target_pairs={{0,1},{1,2},{2,3},{3,4},{4,5},{5,6},{6,7},{7,8},{8,9},{9,10},{10,1... | collective-permute-start | bytes 1179656 | tf_op jit(solution)/shard_map/ppermute | solution.py:26
  222.5 25.5 %collective-permute-start.5 = (bf16[2,96,1024]{2,1,0:T(8,128)(2,1)S(1)}, bf16[2,96,1024]{2,1,0:T(8,128)(2,1)}, u32[]{:S(2)}, u32[]{:S(2)}) collective-permute-start(bf16[2,96,1024]{2,1,0:T(8,128)(2,1)S(1)} %collective-permute-done.4), channel_id=1, source_target_pairs={{0,1},{1,2},{2,3},{3,4},{4,5},{5,6},{6,7},{7,8},{8,9},{9,10},{10,1... | collective-permute-start | bytes 1179656 | tf_op jit(solution)/shard_map/ppermute | solution.py:26
  247.9 22.1 %collective-permute-start.6 = (bf16[2,96,1024]{2,1,0:T(8,128)(2,1)}, bf16[2,96,1024]{2,1,0:T(8,128)(2,1)}, u32[]{:S(2)}, u32[]{:S(2)}) collective-permute-start(bf16[2,96,1024]{2,1,0:T(8,128)(2,1)} %collective-permute-done.5), channel_id=1, source_target_pairs={{0,1},{1,2},{2,3},{3,4},{4,5},{5,6},{6,7},{7,8},{8,9},{9,10},{10,1... | collective-permute-start | bytes 1179656 | tf_op jit(solution)/shard_map/ppermute | solution.py:26
  270.1 21.5 %collective-permute-start.7 = (bf16[2,96,1024]{2,1,0:T(8,128)(2,1)}, bf16[2,96,1024]{2,1,0:T(8,128)(2,1)}, u32[]{:S(2)}, u32[]{:S(2)}) collective-permute-start(bf16[2,96,1024]{2,1,0:T(8,128)(2,1)} %collective-permute-done.6), channel_id=1, source_target_pairs={{0,1},{1,2},{2,3},{3,4},{4,5},{5,6},{6,7},{7,8},{8,9},{9,10},{10,1... | collective-permute-start | bytes 1179656 | tf_op jit(solution)/shard_map/ppermute | solution.py:26
  298.4 1.1 copy-start.1
  298.4 1.3 copy-start.2
  298.7 1.3 copy-start.3
  299.6 1.0 copy-start.4
  300.0 1.0 copy-start.5
Sparse Core Ops, SparseCore 0:
  11.0 77.9 all-gather.2
  92.0 100.8 all-gather.4
where the time goes:
time: 312 us; the launch traced here: 310 us
  waiting for transfers between devices  128 us (41%)
  matrix products  71.3 us (23%)
  local copies, waits for them, and re-layouts  61.4 us (20%)
  starting transfers between devices  23.6 us (8%)
  between operations  14.5 us (5%)
  other arithmetic  9.46 us (3%)
    ppermute x4, waiting for transfers between devices, from_behind(): return lax.ppermute(x, axis, [(i, (i + by) % count) for i in range(count)])  76 us
    ppermute x2, waiting for transfers between devices, extended(): lax.ppermute(lax.slice_in_dim(block, block.shape[dim] - width, None, axis...  27.3 us
    dot_general x16, matrix products, one_head(): jnp.einsum('qd,kd->qk', query_one, key_one, preferred_element_type=jnp.fl...  19.4 us
    dot_general x16, matrix products, one_head(): jnp.dot(weights.astype(jnp.bfloat16), value_one, preferred_element_type=j...  18.6 us
    dot_general x16, matrix products, one_head(): jnp.einsum('ajk,ila->ijlk', bias_lat, lon_table, precision=lax.Precision....  18.3 us
    all_gather x1, waiting for transfers between devices, body(): lax.all_gather(global_weight, 'lat', axis=0, tiled=True)  17.7 us
    dynamic_slice x16, local copies, waits for them, and re-layouts, body(): lax.map(one_head, (jnp.transpose(query_heads, (1, 0, 2)), jnp.transpose(w...  13.2 us
    transpose x16, local copies, waits for them, and re-layouts, one_head(): jnp.einsum('ajk,ila->ijlk', bias_lat, lon_table, precision=lax.Precision....  10.1 us
  transfers between devices with their start and end apart: 10, of which 8 were waited for; matrix products, arithmetic and copies ran while one was open for 41% of the time, Pallas kernels for 0%

commit v1 on v0

--- a/solution.py
+++ b/solution.py
@@ -5,6 +5,12 @@
 from jax.sharding import PartitionSpec as P
 
 STEPS = 4
+
+
+def lay_halves(device_axis, sample):
+    return jnp.concatenate(
+        lax.all_to_all(jnp.stack(lax.axis_size(device_axis) * [sample]), device_axis, 0, 0), 0
+    )
 
 
 def extended(block, sides, width):
@@ -130,7 +136,7 @@
     widened_hidden = hidden.astype(jnp.float32)
     inverse = lax.rsqrt(jnp.mean(widened_hidden * widened_hidden, axis=1, keepdims=True) + 1e-06)
     normed = (widened_hidden * inverse * norm_gain).astype(jnp.bfloat16)
-    triple = fold_rows(normed, lax.all_gather(global_weight, "lat", axis=0, tiled=True))
+    triple = fold_rows(normed, lay_halves("lat", global_weight))
     triple = triple.astype(jnp.bfloat16)
     global_query = triple[:, :model_width].reshape(token_count, head_count, head_size)
     key_pair = jnp.stack([triple[:, model_width : 2 * model_width], triple[:, 2 * model_width :]])

time: 312 us -> 348 us (1.12)
  the two profiles are of different devices: /device:TPU:313 before, /device:TPU:57 now
where the time goes in v1:
time: 348 us; the launch traced here: 346 us
  waiting for transfers between devices  153 us (44%)
  matrix products  70.5 us (20%)
  local copies, waits for them, and re-layouts  65.4 us (19%)
  starting transfers between devices  32.6 us (9%)
  between operations  14.5 us (4%)
  other arithmetic  9.44 us (3%)
    ppermute x4, waiting for transfers between devices, from_behind(): return lax.ppermute(x, axis, [(i, (i + by) % count) for i in range(count)])  82.2 us
    all_gather x1, waiting for transfers between devices, body(): lax.all_gather(output_weight, 'lat', axis=0, tiled=True)  41.2 us
    ppermute x2, waiting for transfers between devices, extended(): lax.ppermute(lax.slice_in_dim(block, 0, width, axis=dim), axis, backward)  27.3 us
    dot_general x16, matrix products, one_head(): jnp.einsum('qd,kd->qk', query_one, key_one, preferred_element_type=jnp.fl...  19.4 us
    dot_general x16, matrix products, one_head(): jnp.dot(weights.astype(jnp.bfloat16), value_one, preferred_element_type=j...  18.6 us
    dot_general x16, matrix products, one_head(): jnp.einsum('ajk,ila->ijlk', bias_lat, lon_table, precision=lax.Precision....  18.3 us
    dynamic_slice x16, local copies, waits for them, and re-layouts, body(): lax.map(one_head, (jnp.transpose(query_heads, (1, 0, 2)), jnp.transpose(w...  13.2 us
    ppermute x2, starting transfers between devices, extended(): lax.ppermute(lax.slice_in_dim(block, 0, width, axis=dim), axis, backward)  12.8 us
  transfers between devices with their start and end apart: 10, of which 9 were waited for; matrix products, arithmetic and copies ran while one was open for 37% of the time, Pallas kernels for 0%

profile of v1, /device:TPU:57, one launch (start us, length us, event | category | flops | bytes accessed | tf_op | source)
XLA Modules:
  0.0 345.9 jit_solution(15131721615536444638)
XLA Ops:
  7.2 1.2 copy_bitcast_fusion.2
  8.6 3.8 %collective-permute-start = (bf16[2,6,8,1024]{3,1,2,0:T(8,128)(2,1)S(1)}, bf16[2,6,8,1024]{3,1,2,0:T(8,128)(2,1)S(1)}, u32[]{:S(2)}, u32[]{:S(2)}) collective-permute-start(bf16[2,6,8,1024]{3,1,2,0:T(8,128)(2,1)S(1)} %get-tuple-element.133), channel_id=1, source_target_pairs={{0,16},{16,32},{32,48},{48,64},{64,80},{80,96},{96,112},{112,128},... | collective-permute-start | bytes 589832 | tf_op jit(solution)/shard_map/ppermute | solution.py:22
  12.4 2.1 collective-permute-start.1
  14.4 1.2 collective-permute-done
  15.6 6.6 %collective-permute-done.1 = bf16[2,6,8,1024]{3,1,2,0:T(8,128)(2,1)S(1)} collective-permute-done((bf16[2,6,8,1024]{3,1,2,0:T(8,128)(2,1)S(1)}, bf16[2,6,8,1024]{3,1,2,0:T(8,128)(2,1)S(1)}, u32[]{:S(2)}, u32[]{:S(2)}) %collective-permute-start.1) | collective-permute-done | bytes 196640 | tf_op jit(solution)/shard_map/ppermute | solution.py:25
  23.6 3.1 collective-permute-start.2
  26.8 10.8 %collective-permute-start.3 = (bf16[2,24,6,1024]{3,1,2,0:T(8,128)(2,1)S(1)}, bf16[2,24,6,1024]{3,1,2,0:T(8,128)(2,1)}, u32[]{:S(2)}, u32[]{:S(2)}) collective-permute-start(bf16[2,24,6,1024]{3,1,2,0:T(8,128)(2,1)S(1)} %get-tuple-element.127), channel_id=1, source_target_pairs={{1,0},{2,1},{3,2},{4,3},{5,4},{6,5},{7,6},{8,7},{9,8},{10,9},{11,1... | collective-permute-start | bytes 1769480 | tf_op jit(solution)/shard_map/ppermute | solution.py:25
  37.6 3.4 stack.17
  41.0 5.0 %all-to-all-start = ((bf16[16,64,3072]{2,1,0:T(8,128)(2,1)}), bf16[16,64,3072]{2,1,0:T(8,128)(2,1)}, u32[]{:S(2)}, u32[]{:S(2)}) async-start(bf16[16,64,3072]{2,1,0:T(8,128)(2,1)} %stack.17), calls=%async_computation | async-start | bytes 12582912 | tf_op jit(solution)/shard_map/all_to_all | solution.py:12
  47.2 20.6 %collective-permute-done.3 = bf16[2,24,6,1024]{3,1,2,0:T(8,128)(2,1)} collective-permute-done((bf16[2,24,6,1024]{3,1,2,0:T(8,128)(2,1)S(1)}, bf16[2,24,6,1024]{3,1,2,0:T(8,128)(2,1)}, u32[]{:S(2)}, u32[]{:S(2)}) %collective-permute-start.3) | collective-permute-done | bytes 589856 | tf_op jit(solution)/shard_map/ppermute | solution.py:25
  67.9 1.6 pad_maximum_fusion
  71.2 1.3 reshape_squeeze.31
  72.5 1.8 copy.88
  74.8 1.3 reshape_squeeze.30
  76.2 1.8 copy.86
  78.0 103.0 %while.11 = (s32[]{:T(128)}, bf16[16,96,64]{1,2,0:T(8,128)(2,1)S(1)}, bf16[16,96,64]{2,1,0:T(8,128)(2,1)S(1)}, bf16[16,480,64]{2,1,0:T(8,128)(2,1)}, f32[16,13,1...) while((s32[]{:T(128)}, ...), condition=%wide.region_5.6_spmd.clone, body=%wide.region_2.5_spmd.clone.sunk | while | flops 19753728 | bytes 2181013 | solution.py:123
  81.9 1.2 fusion.121
  83.3 1.2 fusion.123
  88.3 1.2 fusion.121
  89.7 1.2 fusion.123
  94.7 1.2 fusion.121
  96.1 1.2 fusion.123
  101.2 1.2 fusion.121
  102.6 1.2 fusion.123
  107.6 1.2 fusion.121
  109.0 1.2 fusion.123
  114.0 1.2 fusion.121
  115.5 1.2 fusion.123
  120.5 1.2 fusion.121
  121.9 1.2 fusion.123
  126.9 1.2 fusion.121
  128.3 1.2 fusion.123
  133.3 1.2 fusion.121
  134.8 1.2 fusion.123
  139.8 1.2 fusion.121
  141.2 1.2 fusion.123
  146.2 1.2 fusion.121
  147.6 1.2 fusion.123
  152.7 1.2 fusion.121
  154.1 1.2 fusion.123
  159.1 1.2 fusion.121
  160.5 1.2 fusion.123
  165.5 1.2 fusion.121
  167.0 1.2 fusion.123
  172.0 1.2 fusion.121
  173.4 1.2 fusion.123
  178.4 1.2 fusion.121
  179.8 1.2 fusion.123
  181.0 41.2 %all-gather.2.cloned.1.call-done = bf16[1024,1024]{1,0:T(8,128)(2,1)} async-done(((bf16[64,1024]{1,0:T(8,128)(2,1)}), bf16[1024,1024]{1,0:T(8,128)(2,1)}) %all-gather.2.cloned.1.call-update) | async-done | bytes 2097168 | tf_op jit(solution)/shard_map/all_gather | solution.py:134
  222.3 2.2 fusion.48
  224.5 4.0 %convolution_convert_fusion = bf16[96,3072]{1,0:T(8,128)(2,1)S(1)} fusion(bf16[1024,3072]{1,0:T(8,128)(2,1)} %bitcast.9, bf16[96,1024]{1,0:T(8,128)(2,1)S(1)} %get-tuple-element.147, f32[1024]{0:T(1024)S(1)} %copy-done.11, f32[96]{0:T(128)S(1)} %add_rsqrt_fusion), kind=kOutput, calls=%fused_computation.32 | convolution fusion | flops 604667904 | bytes 7082368 | tf_op jit(solution)/shard_map/dot_general | solution.py:43
  228.7 1.9 collective-permute-start.4
  232.2 22.2 %collective-permute-done.4 = bf16[2,96,1024]{2,1,0:T(8,128)(2,1)S(1)} collective-permute-done((bf16[2,96,1024]{2,1,0:T(8,128)(2,1)S(1)}, bf16[2,96,1024]{2,1,0:T(8,128)(2,1)S(1)}, u32[]{:S(2)}, u32[]{:S(2)}) %collective-permute-start.4) | collective-permute-done | bytes 393248 | tf_op jit(solution)/shard_map/ppermute | solution.py:32
  254.4 1.9 collective-permute-start.5
  257.7 27.1 %collective-permute-done.5 = bf16[2,96,1024]{2,1,0:T(8,128)(2,1)} collective-permute-done((bf16[2,96,1024]{2,1,0:T(8,128)(2,1)S(1)}, bf16[2,96,1024]{2,1,0:T(8,128)(2,1)}, u32[]{:S(2)}, u32[]{:S(2)}) %collective-permute-start.5) | collective-permute-done | bytes 393248 | tf_op jit(solution)/shard_map/ppermute | solution.py:32
  284.8 2.1 collective-permute-start.6
  289.3 16.8 %collective-permute-done.6 = bf16[2,96,1024]{2,1,0:T(8,128)(2,1)} collective-permute-done((bf16[2,96,1024]{2,1,0:T(8,128)(2,1)}, bf16[2,96,1024]{2,1,0:T(8,128)(2,1)}, u32[]{:S(2)}, u32[]{:S(2)}) %collective-permute-start.6) | collective-permute-done | bytes 393248 | tf_op jit(solution)/shard_map/ppermute | solution.py:32
  306.1 1.9 collective-permute-start.7
  310.8 1.3 fusion.85
  312.1 16.0 %collective-permute-done.7 = bf16[2,96,1024]{2,1,0:T(8,128)(2,1)} collective-permute-done((bf16[2,96,1024]{2,1,0:T(8,128)(2,1)}, bf16[2,96,1024]{2,1,0:T(8,128)(2,1)}, u32[]{:S(2)}, u32[]{:S(2)}) %collective-permute-start.7) | collective-permute-done | bytes 393248 | tf_op jit(solution)/shard_map/ppermute | solution.py:32
  328.1 1.8 fusion.80
  329.9 1.8 copy.103
  331.6 1.8 copy.102
  333.4 1.3 fusion.84
  (202 shorter events, 81.4 us)
Async XLA Ops:
  7.2 215.1 %all-gather.2.cloned.1.call-start = ((), (), s32[]{:S(2)}) async-start(), calls=%async_computation.1 | async-start | bytes 2228224 | tf_op jit(solution)/shard_map/all_gather | solution.py:134
  8.6 7.1 %collective-permute-start = (bf16[2,6,8,1024]{3,1,2,0:T(8,128)(2,1)S(1)}, bf16[2,6,8,1024]{3,1,2,0:T(8,128)(2,1)S(1)}, u32[]{:S(2)}, u32[]{:S(2)}) collective-permute-start(bf16[2,6,8,1024]{3,1,2,0:T(8,128)(2,1)S(1)} %get-tuple-element.133), channel_id=1, source_target_pairs={{0,16},{16,32},{32,48},{48,64},{64,80},{80,96},{96,112},{112,128},... | collective-permute-start | bytes 589832 | tf_op jit(solution)/shard_map/ppermute | solution.py:22
  12.3 25.2 %copy-start.6 = (bf16[64,3072]{1,0:T(8,128)(2,1)S(1)}, bf16[64,3072]{1,0:T(8,128)(2,1)}, u32[]{:S(2)}) copy-start(bf16[64,3072]{1,0:T(8,128)(2,1)} %param.17) | copy-start | bytes 1179652
  12.4 9.9 %collective-permute-start.1 = (bf16[2,6,8,1024]{3,1,2,0:T(8,128)(2,1)S(1)}, bf16[2,6,8,1024]{3,1,2,0:T(8,128)(2,1)S(1)}, u32[]{:S(2)}, u32[]{:S(2)}) collective-permute-start(bf16[2,6,8,1024]{3,1,2,0:T(8,128)(2,1)S(1)} %get-tuple-element.134), channel_id=1, source_target_pairs={{16,0},{32,16},{48,32},{64,48},{80,64},{96,80},{112,96},{128,112},... | collective-permute-start | bytes 589832 | tf_op jit(solution)/shard_map/ppermute | solution.py:25
  23.6 23.6 %collective-permute-start.2 = (bf16[2,24,6,1024]{3,1,2,0:T(8,128)(2,1)}, bf16[2,24,6,1024]{3,1,2,0:T(8,128)(2,1)S(1)}, u32[]{:S(2)}, u32[]{:S(2)}) collective-permute-start(bf16[2,24,6,1024]{3,1,2,0:T(8,128)(2,1)} %get-tuple-element.126), channel_id=1, source_target_pairs={{0,1},{1,2},{2,3},{3,4},{4,5},{5,6},{6,7},{7,8},{8,9},{9,10},{10,1... | collective-permute-start | bytes 1769480 | tf_op jit(solution)/shard_map/ppermute | solution.py:22
  26.8 41.1 %collective-permute-start.3 = (bf16[2,24,6,1024]{3,1,2,0:T(8,128)(2,1)S(1)}, bf16[2,24,6,1024]{3,1,2,0:T(8,128)(2,1)}, u32[]{:S(2)}, u32[]{:S(2)}) collective-permute-start(bf16[2,24,6,1024]{3,1,2,0:T(8,128)(2,1)S(1)} %get-tuple-element.127), channel_id=1, source_target_pairs={{1,0},{2,1},{3,2},{4,3},{5,4},{6,5},{7,6},{8,7},{9,8},{10,9},{11,1... | collective-permute-start | bytes 1769480 | tf_op jit(solution)/shard_map/ppermute | solution.py:25
  41.0 5.0 %copy-start.10 = (bf16[12,8,1024]{2,1,0:T(8,128)(2,1)S(1)}, bf16[12,8,1024]{2,1,0:T(8,128)(2,1)}, u32[]{:S(2)}) copy-start(bf16[12,8,1024]{2,1,0:T(8,128)(2,1)} %param.11) | copy-start | bytes 589828
  41.0 183.5 %all-to-all-start = ((bf16[16,64,3072]{2,1,0:T(8,128)(2,1)}), bf16[16,64,3072]{2,1,0:T(8,128)(2,1)}, u32[]{:S(2)}, u32[]{:S(2)}) async-start(bf16[16,64,3072]{2,1,0:T(8,128)(2,1)} %stack.17), calls=%async_computation | async-start | bytes 12582912 | tf_op jit(solution)/shard_map/all_to_all | solution.py:12
  72.5 1.8 copy-start
  76.2 1.8 copy-start.7
  78.0 144.3 %copy-start.9 = (bf16[12,8,1024]{2,1,0:T(8,128)(2,1)S(1)}, bf16[12,8,1024]{2,1,0:T(8,128)(2,1)}, u32[]{:S(2)}) copy-start(bf16[12,8,1024]{2,1,0:T(8,128)(2,1)} %param.10) | copy-start | bytes 589828
  181.0 43.5 %copy-start.11 = (f32[1024]{0:T(1024)S(1)}, f32[1024]{0:T(1024)}, u32[]{:S(2)}) copy-start(f32[1024]{0:T(1024)} %param.16) | copy-start | bytes 12292
  224.5 4.1 %copy-start.5 = (bf16[96,1024]{1,0:T(8,128)(2,1)}, bf16[96,1024]{1,0:T(8,128)(2,1)S(1)}, u32[]{:S(2)}) copy-start(bf16[96,1024]{1,0:T(8,128)(2,1)S(1)} %get-tuple-element.147) | copy-start | bytes 589828
  228.7 25.7 %collective-permute-start.4 = (bf16[2,96,1024]{2,1,0:T(8,128)(2,1)S(1)}, bf16[2,96,1024]{2,1,0:T(8,128)(2,1)S(1)}, u32[]{:S(2)}, u32[]{:S(2)}) collective-permute-start(bf16[2,96,1024]{2,1,0:T(8,128)(2,1)S(1)} %pad_maximum_fusion.2), channel_id=1, source_target_pairs={{0,1},{1,2},{2,3},{3,4},{4,5},{5,6},{6,7},{7,8},{8,9},{9,10},{10,1... | collective-permute-start | bytes 1179656 | tf_op jit(solution)/shard_map/ppermute | solution.py:32
  254.4 30.4 %collective-permute-start.5 = (bf16[2,96,1024]{2,1,0:T(8,128)(2,1)S(1)}, bf16[2,96,1024]{2,1,0:T(8,128)(2,1)}, u32[]{:S(2)}, u32[]{:S(2)}) collective-permute-start(bf16[2,96,1024]{2,1,0:T(8,128)(2,1)S(1)} %collective-permute-done.4), channel_id=1, source_target_pairs={{0,1},{1,2},{2,3},{3,4},{4,5},{5,6},{6,7},{7,8},{8,9},{9,10},{10,1... | collective-permute-start | bytes 1179656 | tf_op jit(solution)/shard_map/ppermute | solution.py:32
  284.8 21.3 %collective-permute-start.6 = (bf16[2,96,1024]{2,1,0:T(8,128)(2,1)}, bf16[2,96,1024]{2,1,0:T(8,128)(2,1)}, u32[]{:S(2)}, u32[]{:S(2)}) collective-permute-start(bf16[2,96,1024]{2,1,0:T(8,128)(2,1)} %collective-permute-done.5), channel_id=1, source_target_pairs={{0,1},{1,2},{2,3},{3,4},{4,5},{5,6},{6,7},{7,8},{8,9},{9,10},{10,1... | collective-permute-start | bytes 1179656 | tf_op jit(solution)/shard_map/ppermute | solution.py:32
  306.1 21.9 %collective-permute-start.7 = (bf16[2,96,1024]{2,1,0:T(8,128)(2,1)}, bf16[2,96,1024]{2,1,0:T(8,128)(2,1)}, u32[]{:S(2)}, u32[]{:S(2)}) collective-permute-start(bf16[2,96,1024]{2,1,0:T(8,128)(2,1)} %collective-permute-done.6), channel_id=1, source_target_pairs={{0,1},{1,2},{2,3},{3,4},{4,5},{5,6},{6,7},{7,8},{8,9},{9,10},{10,1... | collective-permute-start | bytes 1179656 | tf_op jit(solution)/shard_map/ppermute | solution.py:32
  334.7 1.0 copy-start.1
  335.0 1.0 copy-start.2
  335.5 1.0 copy-start.3
  336.0 1.0 copy-start.4
  336.5 1.0 copy-start.8
Sparse Core Ops, SparseCore 0:
  37.7 184.5 all-gather.1
